TPU v7x, 256 devices: a whole 4x4x8 slice. The times are simulated.
256 devices in a mesh: dp: 8 (over z), node: 4 (over x), local: 8 (over y, core).
Axes of the slice: x: 4, y: 4, z: 8, core: 2. Of those that a mesh axis runs over, the one named last changes fastest.
Arguments:
- tokens: bfloat16 [65536, 7168], P(('dp', 'node', 'local')), may hold values from -24 to 24
- cotangent: bfloat16 [65536, 7168], P(('dp', 'node', 'local')), may hold values from -24 to 24
- routes: int32 [65536, 8], P(('dp', 'node', 'local')), may hold values from 0 to 383, all different within a row; in each aligned block of 256 rows (0 to 255, 256 to 511, ...) at most 8 rows name the same one
- probs: bfloat16 [65536, 8], P(('dp', 'node', 'local')), may hold values from 0.049804688 to 0.59765625
- w_gate: bfloat16 [4, 7168, 2048], P('node', 'dp', 'local'), may hold values from -0.0625 to 0.0625
- w_up: bfloat16 [4, 7168, 2048], P('node', 'dp', 'local'), may hold values from -0.0625 to 0.0625
- w_down: bfloat16 [4, 2048, 7168], P('node', 'local', 'dp'), may hold values from -0.125 to 0.125
Outputs:
- token_grad: bfloat16 [65536, 7168], P(('dp', 'node', 'local'))
- router_grad: float32 [65536, 8], P(('dp', 'node', 'local'))
- grad_w_gate: bfloat16 [4, 7168, 2048], P('node', 'dp', 'local')
- grad_w_up: bfloat16 [4, 7168, 2048], P('node', 'dp', 'local')
- grad_w_down: bfloat16 [4, 2048, 7168], P('node', 'local', 'dp')
Inputs may be any that keep to these rules, and one draw needn't show every extreme that they name: `routes`: each row names 8 different experts; among the rows of one device no expert is named more than 8 times, and in every draw some device names some expert exactly 8 times.
All inputs are finite; a program needn't handle non-finite values.
Results may differ from a plain program's by a relative error of at most 0.017.
Values may be sent and summed in bfloat16 or wider, within the bound.
A program may use at most 192 MiB of HBM per device.

v0:
```python
import jax
import jax.numpy as jnp
from jax import lax
from jax.sharding import PartitionSpec as P

ROUTED = 384


def slot_positions(route_rows, experts, capacity):
    flat_routes = route_rows.reshape(-1)
    onehot = (flat_routes[:, None] == jnp.arange(experts, dtype=jnp.int32)[None, :]).astype(
        jnp.int32
    )
    earlier = jnp.cumsum(onehot, axis=0) - onehot
    inside = jnp.sum(onehot, axis=1)
    placed = flat_routes * capacity + jnp.sum(earlier * onehot, axis=1)
    return jnp.where(inside > 0, placed, experts * capacity)


def pack_tokens(values, positions, slots, top_count):
    marks = positions.reshape(values.shape[0], top_count)
    chooser = jnp.sum(
        (marks[None, :, :] == jnp.arange(slots, dtype=jnp.int32)[:, None, None]).astype(jnp.int32),
        axis=2,
    ).astype(values.dtype)
    return jnp.dot(chooser, values, preferred_element_type=jnp.float32).astype(values.dtype)


def pack_routes(values, positions, slots):
    chooser = (positions[None, :] == jnp.arange(slots, dtype=jnp.int32)[:, None]).astype(
        values.dtype
    )
    return jnp.dot(chooser, values, preferred_element_type=jnp.float32).astype(values.dtype)


def expert_terms(rows_in, grads_in, weights_in, gate_slice, up_slice, down_slice):
    gate_value = jnp.dot(rows_in, gate_slice, preferred_element_type=jnp.float32)
    up_value = jnp.dot(rows_in, up_slice, preferred_element_type=jnp.float32)
    sigmoid = jax.nn.sigmoid(gate_value)
    active = gate_value * sigmoid
    hidden = active * up_value
    backed = jnp.dot(grads_in, down_slice.T, preferred_element_type=jnp.float32)
    scales = weights_in.astype(jnp.float32)
    router_part = jnp.sum(backed * hidden, axis=1, keepdims=True)
    grad_hidden = scales * backed
    grad_value = (grad_hidden * active).astype(jnp.bfloat16)
    grad_gate = (grad_hidden * up_value * sigmoid * (1.0 + gate_value * (1.0 - sigmoid))).astype(
        jnp.bfloat16
    )
    weighted = (scales * hidden).astype(jnp.bfloat16)
    token_part = jnp.dot(grad_gate, gate_slice.T, preferred_element_type=jnp.float32) + jnp.dot(
        grad_value, up_slice.T, preferred_element_type=jnp.float32
    )
    return (token_part, router_part, grad_gate, grad_value, weighted)


def per_device(tokens, cotangent, routes, probs, w_gate, w_up, w_down):
    experts = lax.axis_size("node")
    copies = lax.axis_size("local")
    count_rows = tokens.shape[0]
    top_count = routes.shape[1]
    width = tokens.shape[1]
    capacity = 3 * count_rows * top_count // (2 * ROUTED)
    slots = experts * capacity
    sources = experts * copies
    full_gate, full_up = (
        lax.all_gather(w_gate[0], "dp", axis=0, tiled=True),
        lax.all_gather(w_up[0], "dp", axis=0, tiled=True),
    )
    full_down = lax.all_gather(w_down[0], "dp", axis=1, tiled=True)
    positions = slot_positions(routes, experts, capacity)
    packed_tokens = pack_tokens(tokens, positions, slots, top_count).reshape(
        experts, capacity, width
    )
    packed_grads = pack_tokens(cotangent, positions, slots, top_count).reshape(
        experts, capacity, width
    )
    packed_probs = pack_routes(probs.reshape(-1, 1), positions, slots).reshape(experts, capacity, 1)
    spread_tokens = jnp.broadcast_to(
        packed_tokens[:, None], (experts, copies, capacity, width)
    ).reshape(sources, capacity, width)
    spread_grads = jnp.broadcast_to(
        packed_grads[:, None], (experts, copies, capacity, width)
    ).reshape(sources, capacity, width)
    spread_probs = jnp.broadcast_to(packed_probs[:, None], (experts, copies, capacity, 1)).reshape(
        sources, capacity, 1
    )
    got_tokens, got_grads, got_probs = (
        lax.all_to_all(spread_tokens, ("node", "local"), split_axis=0, concat_axis=0, tiled=True),
        lax.all_to_all(spread_grads, ("node", "local"), split_axis=0, concat_axis=0, tiled=True),
        lax.all_to_all(spread_probs, ("node", "local"), split_axis=0, concat_axis=0, tiled=True),
    )
    rows_in = got_tokens.reshape(-1, width)
    grads_in = got_grads.reshape(-1, width)
    weights_in = got_probs.reshape(-1, 1)
    token_part, router_part, grad_gate, grad_value, weighted = expert_terms(
        rows_in, grads_in, weights_in, full_gate, full_up, full_down
    )
    hidden_width = w_gate.shape[2]
    contract = (((0,), (0,)), ((), ()))
    summed = lax.psum_scatter(
        jnp.concatenate(
            [
                lax.dot_general(rows_in, grad_gate, contract, preferred_element_type=jnp.float32),
                lax.dot_general(rows_in, grad_value, contract, preferred_element_type=jnp.float32),
                lax.dot_general(grads_in, weighted, contract, preferred_element_type=jnp.float32),
            ],
            axis=1,
        ).astype(jnp.bfloat16),
        "dp",
        scatter_dimension=0,
        tiled=True,
    ).astype(jnp.float32)
    grad_w_gate = summed[:, :hidden_width].astype(jnp.bfloat16)[None]
    grad_w_up = summed[:, hidden_width : 2 * hidden_width].astype(jnp.bfloat16)[None]
    grad_w_down = summed[:, 2 * hidden_width :].T.astype(jnp.bfloat16)[None]
    back_tokens, back_router = (
        lax.all_to_all(
            token_part.astype(jnp.bfloat16).reshape(sources, capacity, width),
            ("node", "local"),
            split_axis=0,
            concat_axis=0,
            tiled=True,
        ),
        lax.all_to_all(
            router_part.astype(jnp.bfloat16).reshape(sources, capacity, 1),
            ("node", "local"),
            split_axis=0,
            concat_axis=0,
            tiled=True,
        ),
    )
    token_total = jnp.sum(
        back_tokens.astype(jnp.float32).reshape(experts, copies, capacity, width), axis=1
    )
    router_total = jnp.sum(
        back_router.astype(jnp.float32).reshape(experts, copies, capacity, 1), axis=1
    )
    token_table = jnp.concatenate(
        [token_total.reshape(slots, width), jnp.zeros((1, width), jnp.float32)], axis=0
    )
    router_table = jnp.concatenate(
        [router_total.reshape(slots), jnp.zeros((1,), jnp.float32)], axis=0
    )
    picked_tokens = token_table[positions]
    token_grad = jnp.sum(picked_tokens.reshape(count_rows, top_count, width), axis=1).astype(
        jnp.bfloat16
    )
    router_grad = router_table[positions].reshape(count_rows, top_count)
    return (token_grad, router_grad, grad_w_gate, grad_w_up, grad_w_down)


def solution(mesh):
    in_specs = (
        P(("dp", "node", "local"), None),
        P(("dp", "node", "local"), None),
        P(("dp", "node", "local"), None),
        P(("dp", "node", "local"), None),
        P("node", "dp", "local"),
        P("node", "dp", "local"),
        P("node", "local", "dp"),
    )
    out_specs = (
        P(("dp", "node", "local"), None),
        P(("dp", "node", "local"), None),
        P("node", "dp", "local"),
        P("node", "dp", "local"),
        P("node", "local", "dp"),
    )
    return jax.shard_map(
        per_device, mesh=mesh, in_specs=in_specs, out_specs=out_specs, check_vma=False
    )
```

profile of v0, /device:TPU:1, one launch (start us, length us, event | category | flops | bytes accessed | tf_op | source)
XLA Modules:
  0.0 331.5 jit_solution(125044136402110404)
XLA Ops:
  7.2 0.7 all-gather.11.cloned.1.call-update
  7.9 0.7 all-gather.9.cloned.1.call-update
  8.6 0.8 copy.58
  9.5 0.1 eq.58
  9.6 0.1 eq.62
  9.7 0.8 copy.60
  10.5 0.1 reshape.245
  10.6 1.2 reduce-window.6
  11.8 0.2 slice_reduce_fusion
  12.0 0.2 reduce-window.9
  12.4 0.2 fusion.19
  12.5 0.1 broadcast_in_dim.50
  12.6 0.1 copy.61
  12.8 0.1 broadcast_in_dim.52
  12.9 0.7 copy.62
  13.6 8.6 %all-to-all-start = ((bf16[32,8,1]{1,2,0:T(2,128)(2,1)}), bf16[32,8,1]{1,2,0:T(2,128)(2,1)S(1)}, u32[]{:S(2)}, u32[]{:S(2)}) async-start(bf16[32,8,1]{1,2,0:T(2,128)(2,1)} %copy.62), calls=%async_computation | async-start | bytes 32768 | tf_op jit(solution)/shard_map/all_to_all | solution.py:91
  22.2 0.1 reduce_sum.73
  22.3 0.1 gt.23
  22.5 0.1 convert_reduce_fusion.1
  22.6 2.8 fusion.3
  25.4 3.7 %all-to-all-done = bf16[32,8,1]{1,2,0:T(2,128)(2,1)S(1)} async-done(((bf16[32,8,1]{1,2,0:T(2,128)(2,1)}), bf16[32,8,1]{1,2,0:T(2,128)(2,1)S(1)}, u32[]{:S(2)}, u32[]{:S(2)}) %all-to-all-start) | async-done | bytes 544 | tf_op jit(solution)/shard_map/all_to_all | solution.py:91
  29.1 2.3 broadcast_in_dim.57
  31.3 5.1 %all-to-all-start.2 = ((bf16[32,8,7168]{2,1,0:T(8,128)(2,1)}), bf16[32,8,7168]{2,1,0:T(8,128)(2,1)}, u32[]{:S(2)}, u32[]{:S(2)}) async-start(bf16[32,8,7168]{2,1,0:T(8,128)(2,1)} %bitcast.112), calls=%async_computation.2 | async-start | bytes 7340032 | tf_op jit(solution)/shard_map/all_to_all | solution.py:89
  36.4 0.7 all-gather.7.cloned.1.call-update
  37.1 2.8 fusion.2
  39.9 42.5 %all-to-all-done.2 = bf16[32,8,7168]{2,1,0:T(8,128)(2,1)} async-done(((bf16[32,8,7168]{2,1,0:T(8,128)(2,1)}), bf16[32,8,7168]{2,1,0:T(8,128)(2,1)}, u32[]{:S(2)}, u32[]{:S(2)}) %all-to-all-start.2) | async-done | bytes 3670048 | tf_op jit(solution)/shard_map/all_to_all | solution.py:89
  82.4 2.3 broadcast_in_dim.55
  84.7 6.8 %all-to-all-start.1 = ((bf16[32,8,7168]{2,1,0:T(8,128)(2,1)}), bf16[32,8,7168]{2,1,0:T(8,128)(2,1)}, u32[]{:S(2)}, u32[]{:S(2)}) async-start(bf16[32,8,7168]{2,1,0:T(8,128)(2,1)} %bitcast.111), calls=%async_computation.1 | async-start | bytes 7340032 | tf_op jit(solution)/shard_map/all_to_all | solution.py:90
  91.5 0.2 reduce-scatter.4.cloned.1.call-start
  91.8 0.1 reshape.189
  91.9 4.8 %fusion.6 = f32[256,256]{0,1:T(8,128)S(1)} fusion(bf16[1,7168,256]{2,1,0:T(8,128)(2,1)} %all-gather.11.cloned.1.call-done, bf16[32,8,7168]{2,1,0:T(8,128)(2,1)} %all-to-all-done.2), kind=kOutput, calls=%fused_computation.16 | convolution fusion | flops 939524096 | bytes 7602176 | tf_op jit(solution)/shard_map/dot_general | solution.py:37
  96.7 17.2 %all-gather.9.cloned.1.call-done = bf16[1,7168,256]{2,1,0:T(8,128)(2,1)} async-done(((bf16[1,896,256]{2,1,0:T(8,128)(2,1)}), bf16[1,7168,256]{2,1,0:T(8,128)(2,1)}) %all-gather.9.cloned.1.call-update) | async-done | bytes 3670032 | tf_op jit(solution)/shard_map/all_gather | solution.py:68
  113.9 4.7 %fusion.9 = f32[256,256]{0,1:T(8,128)S(1)} fusion(bf16[1,7168,256]{2,1,0:T(8,128)(2,1)} %all-gather.9.cloned.1.call-done, bf16[32,8,7168]{2,1,0:T(8,128)(2,1)} %all-to-all-done.2), kind=kOutput, calls=%fused_computation.19 | convolution fusion | flops 939524096 | bytes 7602176 | tf_op jit(solution)/shard_map/dot_general | solution.py:38
  118.6 19.0 %all-to-all-done.1 = bf16[32,8,7168]{2,1,0:T(8,128)(2,1)} async-done(((bf16[32,8,7168]{2,1,0:T(8,128)(2,1)}), bf16[32,8,7168]{2,1,0:T(8,128)(2,1)}, u32[]{:S(2)}, u32[]{:S(2)}) %all-to-all-start.1) | async-done | bytes 3670048 | tf_op jit(solution)/shard_map/all_to_all | solution.py:90
  137.5 5.1 %convolution_convert_fusion = bf16[7168,256]{0,1:T(8,128)(2,1)} fusion(bf16[32,8,7168]{2,1,0:T(8,128)(2,1)} %all-to-all-done.1, f32[256]{0:T(256)S(1)} %reshape.189, f32[256,256]{0,1:T(8,128)S(1)} %fusion.9, f32[256,256]{0,1:T(8,128)S(1)} %fusion.6), kind=kOutput, calls=%fused_computation.5 | convolution fusion | flops 941817856 | bytes 7865344 | tf_op jit(solution)/shard_map/dot_general | solution.py:106
  142.6 21.6 %all-gather.7.cloned.1.call-done = bf16[1,256,7168]{2,1,0:T(8,128)(2,1)} async-done(((bf16[1,256,896]{2,1,0:T(8,128)(2,1)}), bf16[1,256,7168]{2,1,0:T(8,128)(2,1)}) %all-gather.7.cloned.1.call-update) | async-done | bytes 3670032 | tf_op jit(solution)/shard_map/all_gather | solution.py:70
  164.2 4.4 %multiply_reduce_fusion = (bf16[256]{0:T(256)(128)(2,1)S(1)}, bf16[256,256]{0,1:T(8,128)(2,1)S(1)}, bf16[256,256]{0,1:T(8,128)(2,1)S(1)}) fusion(f32[256,256]{0,1:T(8,128)S(1)} %fusion.9, f32[256,256]{0,1:T(8,128)S(1)} %fusion.6, f32[256]{0:T(256)S(1)} %reshape.189, bf16[1,256,7168]{2,1,0:T(8,128)(2,1)} %all-gather.7.cloned.1.call-done, ...), kind=kOutput, calls=%fused_computation.32 | convolution fusion | flops 940637952 | bytes 8128000 | tf_op jit(solution)/shard_map/dot_general | solution.py:42
  168.6 3.2 convolution_convert_fusion.2
  171.7 3.3 convolution_convert_fusion.1
  175.1 10.9 %pad_maximum_fusion = bf16[7168,768]{0,1:T(8,128)(2,1)} fusion(bf16[7168,256]{0,1:T(8,128)(2,1)S(1)} %copy-done.1, bf16[7168,256]{0,1:T(8,128)(2,1)S(1)} %convolution_convert_fusion.1, bf16[7168,256]{0,1:T(8,128)(2,1)S(1)} %convolution_convert_fusion.2), kind=kLoop, calls=%fused_computation.2 | loop fusion | flops 33030144 | bytes 22020096 | tf_op jit(solution)/shard_map/concatenate | solution.py:102
  185.9 14.6 %copy.71 = bf16[7168,768]{1,0:T(8,128)(2,1)} copy(bf16[7168,768]{0,1:T(8,128)(2,1)} %pad_maximum_fusion) | data formatting | bytes 22020096
  200.6 0.7 convert_element_type.95
  201.3 7.5 %all-to-all-start.4 = ((bf16[32,8,1]{1,2,0:T(2,128)(2,1)}), bf16[32,8,1]{1,2,0:T(2,128)(2,1)S(1)}, u32[]{:S(2)}, u32[]{:S(2)}) async-start(bf16[32,8,1]{1,2,0:T(2,128)(2,1)} %convert_element_type.95), calls=%async_computation.4 | async-start | bytes 32768 | tf_op jit(solution)/shard_map/all_to_all | solution.py:125
  208.9 3.6 %fusion.4 = f32[256,7168]{1,0:T(8,128)S(1)} fusion(bf16[256,256]{0,1:T(8,128)(2,1)S(1)} %get-tuple-element.43, bf16[1,7168,256]{2,1,0:T(8,128)(2,1)} %all-gather.11.cloned.1.call-done), kind=kOutput, calls=%fused_computation.14 | convolution fusion | flops 939524096 | bytes 11141120 | tf_op jit(solution)/shard_map/dot_general | solution.py:51
  212.5 0.5 copy-done
  213.0 3.0 fusion.1
  216.0 7.4 %all-to-all-start.3 = ((bf16[32,8,7168]{2,1,0:T(8,128)(2,1)}), bf16[32,8,7168]{2,1,0:T(8,128)(2,1)}, u32[]{:S(2)}, u32[]{:S(2)}) async-start(bf16[32,8,7168]{2,1,0:T(8,128)(2,1)} %fusion.1), calls=%async_computation.3 | async-start | bytes 7340032 | tf_op jit(solution)/shard_map/all_to_all | solution.py:118
  223.5 0.1 mul.80
  223.8 0.1 reduce_sum.79
  224.0 0.7 fusion.32
  224.7 0.7 fusion.31
  225.5 19.9 %select_select_fusion = f32[2048]{0:T(1024)S(1)} fusion(s32[2048]{0:T(1024)S(1)} %bitcast.119, f32[]{:T(128)} %bitcast.17, f32[]{:T(128)} %bitcast.18, f32[]{:T(128)} %bitcast.19, f32[]{:T(128)} %bitcast.20, f32[]{:T(128)} %bitcast.21, f32[]{:T(128)} %bitcast.22, f32[]{:T(128)} %bitcast.23, f32[]{:T(128)} %bitcast.24, f32[]{:T(128)} %bitcast.25, ...), kind=kLoop, calls=%fused_computation.58 | loop fusion | flops 131072 | bytes 16512 | tf_op jit(solution)/shard_map/gather | solution.py:149
  245.4 0.1 reshape.188
  245.5 0.7 copy.68
  246.2 23.3 %all-to-all-done.3 = bf16[32,8,7168]{2,1,0:T(8,128)(2,1)} async-done(((bf16[32,8,7168]{2,1,0:T(8,128)(2,1)}), bf16[32,8,7168]{2,1,0:T(8,128)(2,1)}, u32[]{:S(2)}, u32[]{:S(2)}) %all-to-all-start.3) | async-done | bytes 3670048 | tf_op jit(solution)/shard_map/all_to_all | solution.py:118
  269.5 2.7 convert_reduce_fusion
  272.3 25.6 %gather_fusion = f32[2048,7168]{1,0:T(8,128)} fusion(f32[33,7168]{1,0:T(8,128)S(1)} %concatenate.10, s32[2048]{0:T(1024)S(1)} %broadcast_clamp_fusion), kind=kCustom, calls=%fused_computation | custom fusion | bytes 117448704 | tf_op jit(solution)/shard_map/gather | solution.py:145
  297.9 22.3 %bitcast_reduce_fusion = bf16[256,7168]{1,0:T(8,128)(2,1)} fusion(f32[2048,7168]{1,0:T(8,128)} %gather_fusion), kind=kLoop, calls=%fused_computation.1 | loop fusion | flops 12845056 | bytes 62390272 | tf_op jit(solution)/shard_map/reduce_sum | solution.py:146
  320.2 1.4 fusion.30
  321.6 1.0 copy.75
  322.5 0.2 copy.74
  322.8 1.0 copy.70
  323.8 0.2 copy.73
  324.0 1.0 copy.69
  (25 shorter events, 1.0 us)
Async XLA Ops:
  7.2 84.8 %all-gather.11.cloned.1.call-start = ((), (), s32[]{:S(2)}) async-start(), calls=%async_computation.8 | async-start | bytes 4128768 | tf_op jit(solution)/shard_map/all_gather | solution.py:67
  7.9 106.0 %all-gather.9.cloned.1.call-start = ((), (), s32[]{:S(2)}) async-start(), calls=%async_computation.7 | async-start | bytes 4128768 | tf_op jit(solution)/shard_map/all_gather | solution.py:68
  13.6 15.5 %all-to-all-start = ((bf16[32,8,1]{1,2,0:T(2,128)(2,1)}), bf16[32,8,1]{1,2,0:T(2,128)(2,1)S(1)}, u32[]{:S(2)}, u32[]{:S(2)}) async-start(bf16[32,8,1]{1,2,0:T(2,128)(2,1)} %copy.62), calls=%async_computation | async-start | bytes 32768 | tf_op jit(solution)/shard_map/all_to_all | solution.py:91
  31.3 51.1 %all-to-all-start.2 = ((bf16[32,8,7168]{2,1,0:T(8,128)(2,1)}), bf16[32,8,7168]{2,1,0:T(8,128)(2,1)}, u32[]{:S(2)}, u32[]{:S(2)}) async-start(bf16[32,8,7168]{2,1,0:T(8,128)(2,1)} %bitcast.112), calls=%async_computation.2 | async-start | bytes 7340032 | tf_op jit(solution)/shard_map/all_to_all | solution.py:89
  36.4 127.8 %all-gather.7.cloned.1.call-start = ((), (), s32[]{:S(2)}) async-start(), calls=%async_computation.6 | async-start | bytes 4128768 | tf_op jit(solution)/shard_map/all_gather | solution.py:70
  84.7 52.8 %all-to-all-start.1 = ((bf16[32,8,7168]{2,1,0:T(8,128)(2,1)}), bf16[32,8,7168]{2,1,0:T(8,128)(2,1)}, u32[]{:S(2)}, u32[]{:S(2)}) async-start(bf16[32,8,7168]{2,1,0:T(8,128)(2,1)} %bitcast.111), calls=%async_computation.1 | async-start | bytes 7340032 | tf_op jit(solution)/shard_map/all_to_all | solution.py:90
  91.5 228.6 %reduce-scatter.4.cloned.1.call-start = ((), (), s32[]{:S(2)}) async-start(), calls=%async_computation.9 | async-start | bytes 12386304
  171.7 3.3 %copy-start.1 = (bf16[7168,256]{0,1:T(8,128)(2,1)S(1)}, bf16[7168,256]{0,1:T(8,128)(2,1)}, u32[]{:S(2)}) copy-start(bf16[7168,256]{0,1:T(8,128)(2,1)} %convolution_convert_fusion) | copy-start | bytes 11010052
  201.3 14.7 %all-to-all-start.4 = ((bf16[32,8,1]{1,2,0:T(2,128)(2,1)}), bf16[32,8,1]{1,2,0:T(2,128)(2,1)S(1)}, u32[]{:S(2)}, u32[]{:S(2)}) async-start(bf16[32,8,1]{1,2,0:T(2,128)(2,1)} %convert_element_type.95), calls=%async_computation.4 | async-start | bytes 32768 | tf_op jit(solution)/shard_map/all_to_all | solution.py:125
  208.9 4.1 %copy-start = (bf16[1,7168,256]{2,1,0:T(8,128)(2,1)S(1)}, bf16[1,7168,256]{2,1,0:T(8,128)(2,1)}, u32[]{:S(2)}) copy-start(bf16[1,7168,256]{2,1,0:T(8,128)(2,1)} %all-gather.9.cloned.1.call-done) | copy-start | bytes 11010052
  216.0 53.4 %all-to-all-start.3 = ((bf16[32,8,7168]{2,1,0:T(8,128)(2,1)}), bf16[32,8,7168]{2,1,0:T(8,128)(2,1)}, u32[]{:S(2)}, u32[]{:S(2)}) async-start(bf16[32,8,7168]{2,1,0:T(8,128)(2,1)} %fusion.1), calls=%async_computation.3 | async-start | bytes 7340032 | tf_op jit(solution)/shard_map/all_to_all | solution.py:118
Sparse Core Ops, SparseCore 0:
  9.8 53.6 all-gather.10
  65.3 48.4 all-gather.8
  115.7 48.5 all-gather.6
  200.7 118.3 reduce-scatter.3
where the time goes:
time: 333 us; the launch traced here: 332 us
  waiting for transfers between devices  129 us (39%)
  other arithmetic  57.6 us (17%)
  local copies, waits for them, and re-layouts  57.1 us (17%)
  matrix products  37.7 us (11%)
  starting transfers between devices  35.8 us (11%)
  between operations  14 us (4%)
    all_to_all x1, waiting for transfers between devices, per_device(): lax.all_to_all(spread_tokens, ('node', 'local'), split_axis=0, concat_axi...  42.5 us
    gather x1, local copies, waits for them, and re-layouts, per_device(): picked_tokens = token_table[positions]  25.6 us
    all_to_all x1, waiting for transfers between devices, per_device(): lax.all_to_all(token_part.astype(jnp.bfloat16).reshape(sources, capacity,...  23.3 us
    reduce_sum x1, other arithmetic, per_device(): jnp.sum(picked_tokens.reshape(count_rows, top_count, width), axis=1)  22.3 us
    all_gather x1, waiting for transfers between devices, per_device(): full_down = lax.all_gather(w_down[0], 'dp', axis=1, tiled=True)  21.6 us
    unnamed x13, local copies, waits for them, and re-layouts  20.9 us
    gather x1, other arithmetic, per_device(): router_grad = router_table[positions].reshape(count_rows, top_count)  19.9 us
    all_to_all x1, waiting for transfers between devices, per_device(): lax.all_to_all(spread_grads, ('node', 'local'), split_axis=0, concat_axis...  19 us
  transfers between devices with their start and end apart: 9, of which 6 were waited for; matrix products, arithmetic and copies ran while one was open for 33% of the time, Pallas kernels for 0%

commit v1 on v0

v1 whole, which is shorter than its diff:
```python
import functools

import jax
import jax.numpy as jnp
from jax import lax
from jax.experimental import pallas as pl
from jax.experimental.pallas import tpu as pltpu
from jax.sharding import PartitionSpec as P

NZ, NX, NY, NC = 8, 4, 4, 2
CAP = 8
BF = jnp.bfloat16
F32 = jnp.float32
MESH = pl.DeviceIdType.MESH
NN = (((1,), (0,)), ((), ()))
NT = (((1,), (1,)), ((), ()))
TN = (((0,), (0,)), ((), ()))
MIB = 1024 * 1024


def dot(a, b, dims=NN):
    return lax.dot_general(a, b, dims, preferred_element_type=F32)


def choose(routes, probs):
    top, rows = routes.shape
    slots = NX * CAP
    place = lax.broadcasted_iota(jnp.int32, (slots, rows), 0)
    expert = jnp.right_shift(place, 3)
    hit = jnp.zeros((slots, rows), F32)
    scale = jnp.zeros((slots, rows), F32)
    for k in range(top):
        same = routes[k : k + 1, :] == expert
        hit = jnp.where(same, 1.0, hit)
        scale = jnp.where(same, probs[k : k + 1, :], scale)
    before = lax.broadcasted_iota(jnp.int32, (rows, rows), 0) < lax.broadcasted_iota(
        jnp.int32, (rows, rows), 1
    )
    earlier = dot(hit.astype(BF), jnp.where(before, 1.0, 0.0).astype(BF))
    slot = jnp.bitwise_and(place, CAP - 1).astype(F32)
    mark = jnp.where(earlier == slot, hit, 0.0)
    return mark.astype(BF), (mark * scale).astype(BF)


def unpack_kernel(
    routes, probs, choice, table, router, gate_in, up_in, down_in,
    token_grad, router_grad, gate_out, up_out, down_out,
    result, gate_v, up_v, down_v, result_s, load_s, grad_s,
):
    top, rows = routes.shape
    slots = NX * CAP
    width = table.shape[3]
    copies = []

    def copy(src, dst, sem):
        started = pltpu.make_async_copy(src, dst, sem)
        started.start()
        copies.append(started)

    through = ((gate_in, gate_v, gate_out), (up_in, up_v, up_out), (down_in, down_v, down_out))
    loads = [pltpu.make_async_copy(src, v, load_s.at[i]) for i, (src, v, _) in enumerate(through)]
    for load in loads:
        load.start()
    chosen = choice[...]
    for d in range(NZ):
        rows_in = table[d].astype(F32).reshape(slots, width).astype(BF)
        result[d] = dot(chosen, rows_in, TN).astype(BF)
        copy(result.at[d], token_grad.at[:, d * width : (d + 1) * width], result_s.at[d])

    for i, (_, v, dst) in enumerate(through):
        loads[i].wait()
        copy(v, dst.at[0], grad_s.at[i])

    values = (router[0] + router[1] + router[2] + router[3])[0:1, 0:slots]
    row, column = (lax.broadcasted_iota(jnp.int32, (slots, slots), i) for i in range(2))
    values = jnp.sum(jnp.where(row == column, values, 0.0), axis=1, keepdims=True)
    spread = chosen.astype(F32) * values
    expert = jnp.right_shift(lax.broadcasted_iota(jnp.int32, (slots, rows), 0), 3)
    named = routes[...]
    place = lax.broadcasted_iota(jnp.int32, (top, rows), 0)
    total = jnp.zeros((top, rows), F32)
    for k in range(top):
        mine = jnp.where(named[k : k + 1, :] == expert, spread, 0.0)
        total = jnp.where(place == k, jnp.sum(mine, axis=0, keepdims=True), total)
    router_grad[...] = total / probs[...].astype(F32)
    for started in copies:
        started.wait()


def unpack(routes, probs, choice, table, router, gate, lift, drop):
    top, rows = routes.shape
    part = table.shape[3]
    width, ff = gate.shape
    vmem = pl.BlockSpec(memory_space=pltpu.VMEM)
    free = pl.BlockSpec(memory_space=pl.ANY)
    return pl.pallas_call(
        unpack_kernel,
        out_shape=(
            jax.ShapeDtypeStruct((rows, NZ * part), BF),
            jax.ShapeDtypeStruct((top, rows), F32),
            jax.ShapeDtypeStruct((1, width, ff), BF),
            jax.ShapeDtypeStruct((1, width, ff), BF),
            jax.ShapeDtypeStruct((1, ff, width), BF),
        ),
        in_specs=[vmem] * 5 + [free] * 3,
        out_specs=(free, vmem, free, free, free),
        scratch_shapes=[
            pltpu.VMEM((NZ, rows, part), BF),
            pltpu.VMEM((width, ff), BF),
            pltpu.VMEM((width, ff), BF),
            pltpu.VMEM((ff, width), BF),
            pltpu.SemaphoreType.DMA((NZ,)),
            pltpu.SemaphoreType.DMA((3,)),
            pltpu.SemaphoreType.DMA((3,)),
        ],
        compiler_params=pltpu.CompilerParams(vmem_limit_bytes=58 * MIB),
    )(routes, probs, choice, table, router, gate, lift, drop)


GROUP_Y = (0, 1, NY - 1, 2)
ORDER = (0, 1, 3, 2)

GAP = 8
STAGES = (
    ("take", 0), ("pass_on", 5), ("near", 7), ("far", 10),
    ("products", 13), ("scatter_1", 17), ("scatter_2", 21), ("scatter_3", 25),
    ("hidden", 29), ("gather_1", 33), ("gather_2", 37), ("gather_3", 41),
    ("tokens", 45), ("weights", 46), ("join", 49), ("relay", 52), ("finish", 55),
)


def expert_kernel(
    routes, probs, tokens_in, cotangent_in, gate_in, up_in, down_in,
    choice, table, router, grad_gate_out, grad_up_out, grad_down_out,
    tokens_v, cotangent_v, w_gate, w_up, w_down, grad_gate, grad_up, grad_down, packed,
    land, rows, part, minus, plus, grads, tokens_out, sibling_in, near_in, far_in, final,
    acc_gate, acc_up, acc_down, tile_z, tile_zin, tile, tile_in, tile_x,
    a2a_s, a2a_r, y_s, y_r, sib_s, sib_r, rs_s, rs_r, ag_s, ag_r, t_s, t_r, yr_s, yr_r,
    back_s, back_r, in_s, w_s, out_s, r0_s, r0_r, r1_s, r1_r, r2_s, r2_r,
):
    z, x, loc = lax.axis_index("dp"), lax.axis_index("node"), lax.axis_index("local")
    y, c = loc // NC, loc % NC
    width = packed.shape[3]
    ff = w_gate.shape[1]
    block = NZ * CAP
    count = NC * NY * block

    def at(dz=0, dx=0, dy=0, dc=0):
        return {
            "dp": (z + dz) % NZ,
            "node": (x + dx) % NX,
            "local": ((y + dy) % NY) * NC + (c + dc) % NC,
        }

    steps_z = (4, 3, 5, 2, 6, 1, 7, 0)
    loads = []
    for dz in steps_z:
        start = pl.multiple_of((z + dz) % NZ * width, 128)
        for i, (src, dst) in enumerate(((tokens_in, tokens_v), (cotangent_in, cotangent_v))):
            load = pltpu.make_async_copy(src.at[:, pl.ds(start, width)], dst.at[dz], in_s.at[i, dz])
            load.start()
            loads.append(load)
    weight_loads = [
        pltpu.make_async_copy(src, dst, w_s.at[i])
        for i, (src, dst) in enumerate(((gate_in, w_gate), (up_in, w_up), (down_in, w_down)))
    ]
    for load in weight_loads:
        load.start()

    sends = []

    def send(src, dst, send_sem, recv_sem, device):
        copy = pltpu.make_async_remote_copy(
            src_ref=src, dst_ref=dst, send_sem=send_sem, recv_sem=recv_sem,
            device_id=device, device_id_type=MESH,
        )
        copy.start()
        sends.append(copy)

    def arrived(dst, recv_sem, device):
        pltpu.make_async_remote_copy(
            src_ref=dst, dst_ref=dst, send_sem=recv_sem, recv_sem=recv_sem,
            device_id=device, device_id_type=MESH,
        ).wait_recv()

    def add(a, b):
        return (a.astype(F32) + b.astype(F32)).astype(BF)

    plane = [(dz, p) for p in ORDER for dz in steps_z if (dz, p) != (0, 0)]
    around = [(k, g) for k in range(NC) for g in range(NY) if (k, g) != (0, 0)]

    barrier = pltpu.get_barrier_semaphore()
    for dz, dx in plane:
        pl.semaphore_signal(barrier, inc=1, device_id=at(dz, dx), device_id_type=MESH)
    for k, g in around:
        pl.semaphore_signal(barrier, inc=1, device_id=at(dy=GROUP_Y[g], dc=k), device_id_type=MESH)
    pick, pick_scaled = choose(routes[...], probs[...].astype(F32))
    choice[...] = pick
    pl.semaphore_wait(barrier, len(plane) + len(around))

    def give(dz, p):
        if (dz, p) == (0, 0):
            land[0, z] = packed[0, x]
            return
        dx, back = (-p) % NX, (-dz) % NZ
        send(
            packed.at[dz, (x + dx) % NX], land.at[p, z],
            a2a_s.at[p, dz], a2a_r.at[p, back], at(dz, dx),
        )

    for i, dz in enumerate(steps_z):
        loads[2 * i].wait()
        loads[2 * i + 1].wait()
        rows_x = dot(pick, tokens_v[dz]).reshape(NX, CAP, width)
        rows_c = dot(pick_scaled, cotangent_v[dz]).reshape(NX, CAP, width)
        packed[dz] = jnp.concatenate([rows_x, rows_c], axis=1).astype(BF)
        give(dz, ORDER[0])
    for p in ORDER[1:]:
        for dz in steps_z:
            give(dz, p)
    for load in weight_loads:
        load.wait()

    up, down, other = at(dy=1), at(dy=NY - 1), at(dc=1)
    zup, zdown = at(dz=1), at(dz=NZ - 1)

    def take(p):
        for dz in range(NZ):
            if (dz, p) != (0, 0):
                arrived(land.at[p, (z + dz) % NZ], a2a_r.at[p, dz], at(dz, p))
        mixed = land[p].astype(F32)
        rows[p, 0, 0, 0] = mixed[:, :CAP].reshape(block, width).astype(BF)
        rows[p, 1, 0, 0] = mixed[:, CAP:].reshape(block, width).astype(BF)
        for h in range(2):
            send(rows.at[p, h, 0, 0], rows.at[p, h, 0, 1], y_s.at[p, 1, h], y_r.at[p, 1, h], down)
            send(
                rows.at[p, 1 - h, 0, 0], rows.at[p, 1 - h, 0, 2],
                y_s.at[p, 2, 1 - h], y_r.at[p, 2, 1 - h], up,
            )
        for h in range(2):
            to_sibling(p, 0, h)

    def to_sibling(p, g, h):
        send(rows.at[p, h, 0, g], rows.at[p, h, 1, g], sib_s.at[p, g, h], sib_r.at[p, g, h], other)

    def from_y(p, g, h):
        arrived(rows.at[p, h, 0, g], y_r.at[p, g, h], up)

    def pass_on(p):
        from_y(p, 1, 0)
        send(rows.at[p, 0, 0, 1], rows.at[p, 0, 0, 3], y_s.at[p, 3, 0], y_r.at[p, 3, 0], down)
        from_y(p, 2, 1)
        send(rows.at[p, 1, 0, 2], rows.at[p, 1, 0, 3], y_s.at[p, 3, 1], y_r.at[p, 3, 1], up)
        to_sibling(p, 1, 0)
        to_sibling(p, 2, 1)

    def near(p):
        from_y(p, 1, 1)
        to_sibling(p, 1, 1)
        from_y(p, 2, 0)
        to_sibling(p, 2, 0)

    def far(p):
        for h in range(2):
            from_y(p, 3, h)
            to_sibling(p, 3, h)

    def products(p):
        for g in range(NY):
            for h in range(2):
                arrived(rows.at[p, h, 1, g], sib_r.at[p, g, h], other)
        in_rows = rows[p, 0].reshape(count, width)
        in_grads = rows[p, 1].reshape(count, width)
        shape = (NZ, block, ff)
        part[p, :, :, 0:ff] = dot(in_rows, w_gate[...]).astype(BF).reshape(shape)
        part[p, :, :, ff : 2 * ff] = dot(in_rows, w_up[...]).astype(BF).reshape(shape)
        part[p, :, :, 2 * ff :] = dot(in_grads, w_down[...], NT).astype(BF).reshape(shape)
        goal = (z + 4) % NZ
        half = block // 2
        send(
            part.at[p, goal, 0:half], minus.at[p, 0, 0:half], rs_s.at[p, 0, 0], rs_r.at[p, 0, 0], zdown
        )
        send(part.at[p, goal, half:], plus.at[p, 0, half:], rs_s.at[p, 1, 0], rs_r.at[p, 1, 0], zup)

    def scatter(p, s):
        low, high = (z + 4 + s) % NZ, (z + 4 - s) % NZ
        half = block // 2
        if s == 1:
            arrived(minus.at[p, 0, 0:half], rs_r.at[p, 0, 0], zup)
            part[p, low, 0:half] = add(part[p, low, 0:half], minus[p, 0, 0:half])
        else:
            arrived(minus.at[p, s - 1], rs_r.at[p, 0, s - 1], zup)
            part[p, low] = add(part[p, low], minus[p, s - 1])
        send(part.at[p, low], minus.at[p, s], rs_s.at[p, 0, s], rs_r.at[p, 0, s], zdown)
        if s == 1:
            arrived(plus.at[p, 0, half:], rs_r.at[p, 1, 0], zdown)
            part[p, high, half:] = add(part[p, high, half:], plus[p, 0, half:])
        else:
            arrived(plus.at[p, s - 1], rs_r.at[p, 1, s - 1], zdown)
            part[p, high] = add(part[p, high], plus[p, s - 1])
        send(part.at[p, high], plus.at[p, s], rs_s.at[p, 1, s], rs_r.at[p, 1, s], zup)

    def hidden(p):
        arrived(minus.at[p, 3], rs_r.at[p, 0, 3], zup)
        arrived(plus.at[p, 3], rs_r.at[p, 1, 3], zdown)
        total = part[p, z].astype(F32) + minus[p, 3].astype(F32) + plus[p, 3].astype(F32)
        gate, lift, back = total[:, :ff], total[:, ff : 2 * ff], total[:, 2 * ff :]
        sigmoid = 1.0 / (1.0 + jnp.exp(-gate))
        active = gate * sigmoid
        value = active * lift
        mine = grads.at[p, z]
        mine[:, 0:ff] = (back * lift * sigmoid * (1.0 + gate * (1.0 - sigmoid))).astype(BF)
        mine[:, ff : 2 * ff] = (back * active).astype(BF)
        mine[:, 2 * ff :] = value.astype(BF)
        send(mine, mine, ag_s.at[p, 1, 0], ag_r.at[p, 1, 0], zup)
        send(mine, mine, ag_s.at[p, 0, 0], ag_r.at[p, 0, 0], zdown)
        terms = back * value
        high = terms.astype(BF)
        rest = (terms - high.astype(F32)).astype(BF)
        ones = jnp.ones((8, ff), BF)
        summed = dot(ones, high, NT) + dot(ones, rest, NT)
        tile_z[p : p + 1, 0:block] = summed[0:1]

    def gather(p, s):
        low, high = grads.at[p, (z + s) % NZ], grads.at[p, (z - s + NZ) % NZ]
        half = block // 2
        arrived(low, ag_r.at[p, 0, s - 1], zup)
        if s < 3:
            send(low, low, ag_s.at[p, 0, s], ag_r.at[p, 0, s], zdown)
        else:
            first = grads.at[p, (z + s) % NZ, 0:half]
            send(first, first, ag_s.at[p, 0, s], ag_r.at[p, 0, s], zdown)
        arrived(high, ag_r.at[p, 1, s - 1], zdown)
        if s < 3:
            send(high, high, ag_s.at[p, 1, s], ag_r.at[p, 1, s], zup)
        else:
            last = grads.at[p, (z - s + NZ) % NZ, half:]
            send(last, last, ag_s.at[p, 1, s], ag_r.at[p, 1, s], zup)

    def tokens(p):
        half = block // 2
        arrived(grads.at[p, (z + 4) % NZ, 0:half], ag_r.at[p, 0, 3], zup)
        arrived(grads.at[p, (z + 4) % NZ, half:], ag_r.at[p, 1, 3], zdown)
        for k in (1, 0):
            both = grads[p, k * NY : (k + 1) * NY].reshape(NY * block, 3 * ff)
            value = dot(both[:, :ff], w_gate[...], NT) + dot(both[:, ff : 2 * ff], w_up[...], NT)
            tokens_out[p, k] = value.astype(BF).reshape(NY, block, width)
            if k == 1:
                send(tokens_out.at[p, 1], sibling_in.at[p], t_s.at[p], t_r.at[p], other)

    stores = [
        pltpu.make_async_copy(src, dst, out_s.at[i])
        for i, (src, dst) in enumerate(
            ((grad_gate, grad_gate_out), (grad_up, grad_up_out), (grad_down, grad_down_out))
        )
    ]

    def weights(p):
        both = grads[p].reshape(count, 3 * ff)
        in_rows = rows[p, 0].reshape(count, width)
        in_grads = rows[p, 1].reshape(count, width)
        gate = dot(in_rows, both[:, :ff], TN)
        lift = dot(in_rows, both[:, ff : 2 * ff], TN)
        drop = dot(both[:, 2 * ff :], in_grads, TN)
        if p == ORDER[0]:
            acc_gate[...], acc_up[...], acc_down[...] = gate, lift, drop
        elif p != ORDER[-1]:
            acc_gate[...] += gate
            acc_up[...] += lift
            acc_down[...] += drop
        else:
            grad_gate[...] = (acc_gate[...] + gate).astype(BF)
            grad_up[...] = (acc_up[...] + lift).astype(BF)
            grad_down[...] = (acc_down[...] + drop).astype(BF)
            for copy in stores:
                copy.start()

    def join(p):
        half = block // 2
        arrived(sibling_in.at[p], t_r.at[p], other)
        tokens_out[p, 0] = add(tokens_out[p, 0], sibling_in[p])
        send(tokens_out.at[p, 0, 3, 0:half], far_in.at[p, 0], yr_s.at[p, 0], yr_r.at[p, 0], up)
        send(tokens_out.at[p, 0, 3, half:], far_in.at[p, 1], yr_s.at[p, 1], yr_r.at[p, 1], down)

    def relay(p):
        half = block // 2
        arrived(far_in.at[p, 0], yr_r.at[p, 0], down)
        tokens_out[p, 0, 1, 0:half] = add(tokens_out[p, 0, 1, 0:half], far_in[p, 0])
        send(tokens_out.at[p, 0, 1], near_in.at[p, 0], yr_s.at[p, 2], yr_r.at[p, 2], up)
        arrived(far_in.at[p, 1], yr_r.at[p, 1], up)
        tokens_out[p, 0, 2, half:] = add(tokens_out[p, 0, 2, half:], far_in[p, 1])
        send(tokens_out.at[p, 0, 2], near_in.at[p, 1], yr_s.at[p, 3], yr_r.at[p, 3], down)

    def finish(p):
        arrived(near_in.at[p, 0], yr_r.at[p, 2], down)
        arrived(near_in.at[p, 1], yr_r.at[p, 3], up)
        value = tokens_out[p, 0, 0].astype(F32) + near_in[p, 0].astype(F32) + near_in[p, 1].astype(F32)
        final[p] = value.reshape(NZ, CAP, width).astype(BF)
        for dz in steps_z:
            if (dz, p) != (0, 0):
                send(
                    final.at[p, (z + dz) % NZ], table.at[z, x],
                    back_s.at[p, dz], back_r.at[(-p) % NX, (-dz) % NZ], at(dz, p),
                )
            else:
                table[z, x] = final[p, z]

    others_z = range(1, NZ)

    def router_start():
        for dz in others_z:
            send(tile_z, tile_zin.at[z], r0_s.at[dz], r0_r.at[(-dz) % NZ], at(dz))
        tile_zin[z] = tile_z[...]

    def three_parts(value):
        top = value.astype(BF)
        middle = (value - top.astype(F32)).astype(BF)
        low = (value - top.astype(F32) - middle.astype(F32)).astype(BF)
        return top, middle, low

    def moved(value, source, goal):
        move = jnp.where(source & goal, 1.0, 0.0).astype(BF)
        top, middle, low = three_parts(value)
        return dot(top, move) + dot(middle, move) + dot(low, move)

    row = lax.broadcasted_iota(jnp.int32, (128, 128), 0)
    column = lax.broadcasted_iota(jnp.int32, (128, 128), 1)
    in_slot = jnp.bitwise_and(row, CAP - 1)

    def router_local():
        for dz in others_z:
            arrived(tile_zin.at[(z + dz) % NZ], r0_r.at[dz], at(dz))
        total = jnp.zeros((8, 128), F32)
        inside = lax.broadcasted_iota(jnp.int32, (8, 128), 1) < block
        for p in range(NX):
            value = jnp.concatenate([tile_zin[b, p : p + 1, :] for b in range(NZ)], axis=0)
            value = jnp.where(inside, value, 0.0)
            total = total + moved(value, jnp.right_shift(row, 3) == z, column == p * CAP + in_slot)
        tile[...] = total
        for k, g in around:
            i = NY * k + g
            send(tile, tile_in.at[i], r1_s.at[i], r1_r.at[i], at(dy=GROUP_Y[g], dc=k))

    def router_x():
        summed = tile[0:1, :]
        for k, g in around:
            i = NY * k + g
            arrived(tile_in.at[i], r1_r.at[i], other)
            summed = summed + tile_in[i, i : i + 1, :]
        wide = jnp.broadcast_to(summed, (8, 128))
        for dx in range(NX):
            tile_x[dx] = moved(wide, jnp.right_shift(row, 3) == dx, column == x * CAP + in_slot)
        router[x] = tile_x[0]
        for dx in range(1, NX):
            send(tile_x.at[dx], router.at[x], r2_s.at[dx], r2_r.at[(-dx) % NX], at(dx=dx))

    todo = {
        "take": take, "pass_on": pass_on, "near": near, "far": far, "products": products,
        "hidden": hidden, "tokens": tokens, "weights": weights, "join": join, "relay": relay,
        "finish": finish,
    }
    for s in (1, 2, 3):
        todo[f"scatter_{s}"] = functools.partial(scatter, s=s)
        todo[f"gather_{s}"] = functools.partial(gather, s=s)
    plan = [
        (start + place * GAP, place, stage, p)
        for place, p in enumerate(ORDER)
        for stage, start in STAGES
    ]
    last = {stage: start + (NX - 1) * GAP for stage, start in STAGES}
    plan.append((last["hidden"] + 0.1, NX, router_start, None))
    plan.append((last["gather_2"] + 0.1, NX, router_local, None))
    plan.append((last["tokens"] + 0.1, NX, router_x, None))
    for _, _, stage, p in sorted(plan, key=lambda item: item[:2]):
        if p is None:
            stage()
        else:
            todo[stage](p)

    for dx in range(1, NX):
        arrived(router.at[(x + dx) % NX], r2_r.at[dx], at(dx=dx))
    for p in ORDER:
        for dz in range(NZ):
            if (dz, p) != (0, 0):
                arrived(table.at[(z + dz) % NZ, (x + p) % NX], back_r.at[p, dz], at(dz, p))
    for copy in stores:
        copy.wait()
    for copy in sends:
        copy.wait_send()


def experts(routes, probs, tokens, cotangent, w_gate, w_up, w_down):
    width, ff = w_gate.shape
    count = tokens.shape[0]
    block = NZ * CAP
    vmem = pl.BlockSpec(memory_space=pltpu.VMEM)
    free = pl.BlockSpec(memory_space=pl.ANY)
    dma = lambda *shape: pltpu.SemaphoreType.DMA(shape)
    flops = 2 * 8 * NX * NC * NY * block * width * ff
    return pl.pallas_call(
        expert_kernel,
        out_shape=(
            jax.ShapeDtypeStruct((NX * CAP, count), BF),
            jax.ShapeDtypeStruct((NZ, NX, CAP, width), BF),
            jax.ShapeDtypeStruct((NX, 8, 128), F32),
            jax.ShapeDtypeStruct((width, ff), BF),
            jax.ShapeDtypeStruct((width, ff), BF),
            jax.ShapeDtypeStruct((ff, width), BF),
        ),
        in_specs=[vmem] * 2 + [free] * 5,
        out_specs=(vmem,) * 3 + (free,) * 3,
        scratch_shapes=[
            pltpu.VMEM((NZ, count, width), BF),
            pltpu.VMEM((NZ, count, width), BF),
            pltpu.VMEM((width, ff), BF),
            pltpu.VMEM((width, ff), BF),
            pltpu.VMEM((ff, width), BF),
            pltpu.VMEM((width, ff), BF),
            pltpu.VMEM((width, ff), BF),
            pltpu.VMEM((ff, width), BF),
            pltpu.VMEM((NZ, NX, 2 * CAP, width), BF),
            pltpu.VMEM((NX, NZ, 2 * CAP, width), BF),
            pltpu.VMEM((NX, 2, NC, NY, block, width), BF),
            pltpu.VMEM((NX, NZ, block, 3 * ff), BF),
            pltpu.VMEM((NX, 4, block, 3 * ff), BF),
            pltpu.VMEM((NX, 4, block, 3 * ff), BF),
            pltpu.VMEM((NX, NZ, block, 3 * ff), BF),
            pltpu.VMEM((NX, NC, NY, block, width), BF),
            pltpu.VMEM((NX, NY, block, width), BF),
            pltpu.VMEM((NX, 2, block, width), BF),
            pltpu.VMEM((NX, 2, block // 2, width), BF),
            pltpu.VMEM((NX, NZ, CAP, width), BF),
            pltpu.VMEM((width, ff), F32),
            pltpu.VMEM((width, ff), F32),
            pltpu.VMEM((ff, width), F32),
            pltpu.VMEM((8, 128), F32),
            pltpu.VMEM((NZ, 8, 128), F32),
            pltpu.VMEM((8, 128), F32),
            pltpu.VMEM((8, 8, 128), F32),
            pltpu.VMEM((NX, 8, 128), F32),
            dma(NX, NZ), dma(NX, NZ), dma(NX, NY, 2), dma(NX, NY, 2), dma(NX, NY, 2), dma(NX, NY, 2),
            dma(NX, 2, 4), dma(NX, 2, 4), dma(NX, 2, 4), dma(NX, 2, 4),
            dma(NX), dma(NX), dma(NX, 4), dma(NX, 4),
            dma(NX, NZ), dma(NX, NZ), dma(2, NZ), dma(3), dma(3), dma(NZ), dma(NZ), dma(8), dma(8), dma(NX), dma(NX),
        ],
        compiler_params=pltpu.CompilerParams(
            collective_id=0, has_side_effects=True, vmem_limit_bytes=56 * MIB
        ),
        cost_estimate=pl.CostEstimate(flops=flops, bytes_accessed=16 * MIB, transcendentals=0),
    )(routes, probs, tokens, cotangent, w_gate, w_up, w_down)


def per_device(tokens, cotangent, routes, probs, w_gate, w_up, w_down):
    routes, probs = routes.T, probs.T
    choice, table, router, gate, lift, drop = experts(
        routes, probs, tokens, cotangent, w_gate[0], w_up[0], w_down[0]
    )
    token_grad, router_grad, gate, lift, drop = unpack(
        routes, probs, choice, table, router, gate, lift, drop
    )
    return token_grad, router_grad.T, gate, lift, drop


def solution(mesh):
    split = P(("dp", "node", "local"), None)
    specs = (P("node", "dp", "local"), P("node", "dp", "local"), P("node", "local", "dp"))
    return jax.shard_map(
        per_device,
        mesh=mesh,
        in_specs=(split,) * 4 + specs,
        out_specs=(split,) * 2 + specs,
        check_vma=False,
    )
```

time: 333 us -> 138 us (0.41)
  Pallas kernels: 0 us -> 134 us
  waiting for transfers between devices: 129 us -> 0 us
  other arithmetic: 57.6 us -> 0 us
  local copies, waits for them, and re-layouts: 57.1 us -> 0 us
  matrix products: 37.7 us -> 0 us
  starting transfers between devices: 35.8 us -> 0 us
  between operations: 14 us -> 0.8 us
    pallas_call x0 -> x2, Pallas kernels: none -> 134 us  [the longest x1 129 us: experts(): pl.pallas_call(expert_kernel, out_shape=(jax.ShapeDtypeStruct((NX * CAP,...]
    all_to_all x5 -> x0, waiting for transfers between devices: 88.5 us -> none  [the longest x1 42.5 us: per_device(): lax.all_to_all(spread_tokens, ('node', 'local'), split_axis=0, concat_axi...]
    all_gather x3 -> x0, waiting for transfers between devices: 38.8 us -> none  [the longest x1 21.6 us: per_device(): full_down = lax.all_gather(w_down[0], 'dp', axis=1, tiled=True)]
    dot_general x11 -> x0, matrix products: 37.7 us -> none  [the longest x2 5.59 us: pack_tokens(): jnp.dot(chooser, values, preferred_element_type=jnp.float32)]
    all_to_all x5 -> x0, starting transfers between devices: 35.5 us -> none  [the longest x1 8.59 us: per_device(): lax.all_to_all(spread_probs, ('node', 'local'), split_axis=0, concat_axis...]
    gather x3 -> x0, local copies, waits for them, and re-layouts: 27 us -> none  [the longest x1 25.6 us: per_device(): picked_tokens = token_table[positions]]
    reduce_sum x5 -> x0, other arithmetic: 25.3 us -> none  [the longest x1 22.3 us: per_device(): jnp.sum(picked_tokens.reshape(count_rows, top_count, width), axis=1)]
    unnamed x13 -> x0, local copies, waits for them, and re-layouts: 20.9 us -> none
  transfers between devices with their start and end apart: 9 -> 0, of which waited for: 6 -> 0; matrix products, arithmetic and copies ran while one was open for 33% -> 0% of each run, Pallas kernels for 0% -> 0%
where the time goes in v1:
time: 138 us; the launch traced here: 135 us
  Pallas kernels  134 us (97%)
    pallas_call x1, Pallas kernels, experts(): pl.pallas_call(expert_kernel, out_shape=(jax.ShapeDtypeStruct((NX * CAP,...  129 us
    pallas_call x1, Pallas kernels, unpack(): pl.pallas_call(unpack_kernel, out_shape=(jax.ShapeDtypeStruct((rows, NZ *...  5.5 us

profile of v1, /device:TPU:1, one launch (start us, length us, event | category | flops | bytes accessed | tf_op | source)
XLA Modules:
  0.0 135.3 jit_solution(10251268423902324750)
XLA Ops:
  0.6 129.0 %shard_map.110 = (bf16[32,256]{1,0:T(8,128)(2,1)}, bf16[8,4,8,896]{3,2,1,0:T(8,128)(2,1)}, f32[4,8,128]{2,1,0:T(8,128)}, bf16[896,256]{1,0:T(8,128)(2,1)}, bf16[...) custom-call(s32[8,256]{1,0:T(8,128)} %bitcast.6, bf16[8,256]{1,0:T(8,128)(2,1)} %bitcast.8, bf16[256,7168]{1,0:T(8,128)(2,1)} %tokens_in.1, ...), custom_call_target="tpu_custom_call" | custom-call | flops 7516192768 | bytes 16777216 | tf_op jit(solution)/shard_map/pallas_call | solution.py:500
  129.6 5.5 %shard_map.111 = (bf16[256,7168]{1,0:T(8,128)(2,1)}, f32[8,256]{1,0:T(8,128)}, bf16[1,896,256]{2,1,0:T(8,128)(2,1)}, bf16[1,896,256]{2,1,0:T(8,128)(2,1)}, bf16[1,256,896]{2,1,0:T(8,128)(2,1)}) custom-call(s32[8,256]{1,0:T(8,128)} %bitcast.7, bf16[8,256]{1,0:T(8,128)(2,1)} %bitcast.9, bf16[32,256]{1,0:T(8,128)(2,1)} %get-tuple-element.16.choice, ...), custom_call_target="tpu_custom_call" | custom-call | tf_op jit(solution)/shard_map/pallas_call | solution.py:96

commit v2 on v1

--- a/solution.py
+++ b/solution.py
@@ -120,27 +120,48 @@
 GROUP_Y = (0, 1, NY - 1, 2)
 ORDER = (0, 1, 3, 2)
 
-GAP = 8
 STAGES = (
-    ("take", 0), ("pass_on", 5), ("near", 7), ("far", 10),
-    ("products", 13), ("scatter_1", 17), ("scatter_2", 21), ("scatter_3", 25),
-    ("hidden", 29), ("gather_1", 33), ("gather_2", 37), ("gather_3", 41),
-    ("tokens", 45), ("weights", 46), ("join", 49), ("relay", 52), ("finish", 55),
+    ("take", 0, 3, 13, 23),
+    ("pass_tokens", 1, 9, 19, 34),
+    ("pass_grads", 2, 10, 22, 35),
+    ("near_grads", 5, 11, 24, 46),
+    ("near_tokens", 4, 12, 27, 38),
+    ("far_tokens", 6, 16, 31, 41),
+    ("far_grads", 7, 17, 30, 42),
+    ("products", 8, 18, 36, 48),
+    ("scatter_down_1", 14, 25, 43, 52),
+    ("scatter_up_1", 15, 26, 44, 56),
+    ("scatter_down_2", 21, 32, 53, 59),
+    ("scatter_up_2", 20, 33, 54, 62),
+    ("scatter_down_3", 28, 39, 61, 65),
+    ("scatter_up_3", 29, 40, 60, 67),
+    ("hidden", 37, 49, 68, 73),
+    ("gather_down_1", 45, 55, 74, 77),
+    ("gather_up_1", 47, 58, 75, 78),
+    ("gather_down_2", 50, 63, 81, 83),
+    ("gather_up_2", 51, 64, 82, 84),
+    ("gather_down_3", 57, 70, 87, 91),
+    ("gather_up_3", 66, 71, 89, 92),
+    ("tokens", 72, 76, 93, 94),
+    ("weights", 69, 104, 106, 107),
+    ("join", 80, 79, 95, 97),
+    ("relay_up", 85, 88, 98, 102),
+    ("relay_down", 86, 90, 99, 101),
+    ("finish", 96, 100, 103, 105),
 )
 
 
 def expert_kernel(
     routes, probs, tokens_in, cotangent_in, gate_in, up_in, down_in,
     choice, table, router, grad_gate_out, grad_up_out, grad_down_out,
-    tokens_v, cotangent_v, w_gate, w_up, w_down, grad_gate, grad_up, grad_down, packed,
+    inputs, w_gate, w_up, w_down, grad_gate, grad_up, grad_down, packed,
     land, rows, part, minus, plus, grads, tokens_out, sibling_in, near_in, far_in, final,
     acc_gate, acc_up, acc_down, tile_z, tile_zin, tile, tile_in, tile_x,
-    a2a_s, a2a_r, y_s, y_r, sib_s, sib_r, rs_s, rs_r, ag_s, ag_r, t_s, t_r, yr_s, yr_r,
-    back_s, back_r, in_s, w_s, out_s, r0_s, r0_r, r1_s, r1_r, r2_s, r2_r,
+    sent, a2a_r, y_r, sib_r, rs_r, ag_r, t_r, yr_r, back_r, in_s, w_s, out_s, router_r,
 ):
     z, x, loc = lax.axis_index("dp"), lax.axis_index("node"), lax.axis_index("local")
     y, c = loc // NC, loc % NC
-    width = packed.shape[3]
+    width = packed.shape[2]
     ff = w_gate.shape[1]
     block = NZ * CAP
     count = NC * NY * block
@@ -153,13 +174,12 @@
         }
 
     steps_z = (4, 3, 5, 2, 6, 1, 7, 0)
-    loads = []
     for dz in steps_z:
         start = pl.multiple_of((z + dz) % NZ * width, 128)
-        for i, (src, dst) in enumerate(((tokens_in, tokens_v), (cotangent_in, cotangent_v))):
-            load = pltpu.make_async_copy(src.at[:, pl.ds(start, width)], dst.at[dz], in_s.at[i, dz])
-            load.start()
-            loads.append(load)
+        for i, src in enumerate((tokens_in, cotangent_in)):
+            pltpu.make_async_copy(
+                src.at[:, pl.ds(start, width)], inputs.at[dz, i], in_s.at[dz]
+            ).start()
     weight_loads = [
         pltpu.make_async_copy(src, dst, w_s.at[i])
         for i, (src, dst) in enumerate(((gate_in, w_gate), (up_in, w_up), (down_in, w_down)))
@@ -167,15 +187,19 @@
     for load in weight_loads:
         load.start()
 
-    sends = []
-
-    def send(src, dst, send_sem, recv_sem, device):
-        copy = pltpu.make_async_remote_copy(
-            src_ref=src, dst_ref=dst, send_sem=send_sem, recv_sem=recv_sem,
+    kinds = ("a2a", "y", "sibling", "scatter", "gather", "terms", "sums", "back", "rz", "ry", "rx")
+
+    def send(src, dst, kind, recv_sem, device):
+        pltpu.make_async_remote_copy(
+            src_ref=src, dst_ref=dst, send_sem=sent.at[kinds.index(kind)], recv_sem=recv_sem,
             device_id=device, device_id_type=MESH,
-        )
-        copy.start()
-        sends.append(copy)
+        ).start()
+
+    def all_sent(kind, same_bytes):
+        pltpu.make_async_remote_copy(
+            src_ref=same_bytes, dst_ref=same_bytes, send_sem=sent.at[kinds.index(kind)],
+            recv_sem=back_r, device_id=at(dz=1), device_id_type=MESH,
+        ).wait_send()
 
     def arrived(dst, recv_sem, device):
         pltpu.make_async_remote_copy(
@@ -200,20 +224,16 @@
 
     def give(dz, p):
         if (dz, p) == (0, 0):
-            land[0, z] = packed[0, x]
+            land[0, z] = packed[x]
             return
-        dx, back = (-p) % NX, (-dz) % NZ
-        send(
-            packed.at[dz, (x + dx) % NX], land.at[p, z],
-            a2a_s.at[p, dz], a2a_r.at[p, back], at(dz, dx),
-        )
-
-    for i, dz in enumerate(steps_z):
-        loads[2 * i].wait()
-        loads[2 * i + 1].wait()
-        rows_x = dot(pick, tokens_v[dz]).reshape(NX, CAP, width)
-        rows_c = dot(pick_scaled, cotangent_v[dz]).reshape(NX, CAP, width)
-        packed[dz] = jnp.concatenate([rows_x, rows_c], axis=1).astype(BF)
+        dx = (-p) % NX
+        send(packed.at[dz * NX + (x + dx) % NX], land.at[p, z], "a2a", a2a_r.at[p], at(dz, dx))
+
+    for dz in steps_z:
+        pltpu.make_async_copy(inputs.at[dz], inputs.at[dz], in_s.at[dz]).wait()
+        rows_x = dot(pick, inputs[dz, 0]).reshape(NX, CAP, width)
+        rows_c = dot(pick_scaled, inputs[dz, 1]).reshape(NX, CAP, width)
+        packed[dz * NX : (dz + 1) * NX] = jnp.concatenate([rows_x, rows_c], axis=1).astype(BF)
         give(dz, ORDER[0])
     for p in ORDER[1:]:
         for dz in steps_z:
@@ -225,50 +245,38 @@
     zup, zdown = at(dz=1), at(dz=NZ - 1)
 
     def take(p):
-        for dz in range(NZ):
-            if (dz, p) != (0, 0):
-                arrived(land.at[p, (z + dz) % NZ], a2a_r.at[p, dz], at(dz, p))
+        arrived(land.at[p, (1 if p == 0 else 0) : NZ], a2a_r.at[p], zup)
         mixed = land[p].astype(F32)
         rows[p, 0, 0, 0] = mixed[:, :CAP].reshape(block, width).astype(BF)
         rows[p, 1, 0, 0] = mixed[:, CAP:].reshape(block, width).astype(BF)
         for h in range(2):
-            send(rows.at[p, h, 0, 0], rows.at[p, h, 0, 1], y_s.at[p, 1, h], y_r.at[p, 1, h], down)
-            send(
-                rows.at[p, 1 - h, 0, 0], rows.at[p, 1 - h, 0, 2],
-                y_s.at[p, 2, 1 - h], y_r.at[p, 2, 1 - h], up,
-            )
+            send(rows.at[p, h, 0, 0], rows.at[p, h, 0, 1], "y", y_r.at[p, 0, h], down)
+            send(rows.at[p, 1 - h, 0, 0], rows.at[p, 1 - h, 0, 2], "y", y_r.at[p, 1, 1 - h], up)
         for h in range(2):
             to_sibling(p, 0, h)
 
     def to_sibling(p, g, h):
-        send(rows.at[p, h, 0, g], rows.at[p, h, 1, g], sib_s.at[p, g, h], sib_r.at[p, g, h], other)
+        send(rows.at[p, h, 0, g], rows.at[p, h, 1, g], "sibling", sib_r.at[p], other)
 
     def from_y(p, g, h):
-        arrived(rows.at[p, h, 0, g], y_r.at[p, g, h], up)
-
-    def pass_on(p):
+        arrived(rows.at[p, h, 0, g], y_r.at[p, g - 1, h], up)
+
+    def pass_tokens(p):
         from_y(p, 1, 0)
-        send(rows.at[p, 0, 0, 1], rows.at[p, 0, 0, 3], y_s.at[p, 3, 0], y_r.at[p, 3, 0], down)
+        send(rows.at[p, 0, 0, 1], rows.at[p, 0, 0, 3], "y", y_r.at[p, 2, 0], down)
+        to_sibling(p, 1, 0)
+
+    def pass_grads(p):
         from_y(p, 2, 1)
-        send(rows.at[p, 1, 0, 2], rows.at[p, 1, 0, 3], y_s.at[p, 3, 1], y_r.at[p, 3, 1], up)
-        to_sibling(p, 1, 0)
+        send(rows.at[p, 1, 0, 2], rows.at[p, 1, 0, 3], "y", y_r.at[p, 2, 1], up)
         to_sibling(p, 2, 1)
 
-    def near(p):
-        from_y(p, 1, 1)
-        to_sibling(p, 1, 1)
-        from_y(p, 2, 0)
-        to_sibling(p, 2, 0)
-
-    def far(p):
-        for h in range(2):
-            from_y(p, 3, h)
-            to_sibling(p, 3, h)
+    def keep(p, g, h):
+        from_y(p, g, h)
+        to_sibling(p, g, h)
 
     def products(p):
-        for g in range(NY):
-            for h in range(2):
-                arrived(rows.at[p, h, 1, g], sib_r.at[p, g, h], other)
+        arrived(rows.at[p, :, 1], sib_r.at[p], other)
         in_rows = rows[p, 0].reshape(count, width)
         in_grads = rows[p, 1].reshape(count, width)
         shape = (NZ, block, ff)
@@ -278,12 +286,12 @@
         goal = (z + 4) % NZ
         half = block // 2
         send(
-            part.at[p, goal, 0:half], minus.at[p, 0, 0:half], rs_s.at[p, 0, 0], rs_r.at[p, 0, 0], zdown
+            part.at[p, goal, 0:half], minus.at[p, 0, 0:half], "scatter", rs_r.at[p, 0, 0], zdown
         )
-        send(part.at[p, goal, half:], plus.at[p, 0, half:], rs_s.at[p, 1, 0], rs_r.at[p, 1, 0], zup)
-
-    def scatter(p, s):
-        low, high = (z + 4 + s) % NZ, (z + 4 - s) % NZ
+        send(part.at[p, goal, half:], plus.at[p, 0, half:], "scatter", rs_r.at[p, 1, 0], zup)
+
+    def scatter_down(p, s):
+        low = (z + 4 + s) % NZ
         half = block // 2
         if s == 1:
             arrived(minus.at[p, 0, 0:half], rs_r.at[p, 0, 0], zup)
@@ -291,14 +299,18 @@
         else:
             arrived(minus.at[p, s - 1], rs_r.at[p, 0, s - 1], zup)
             part[p, low] = add(part[p, low], minus[p, s - 1])
-        send(part.at[p, low], minus.at[p, s], rs_s.at[p, 0, s], rs_r.at[p, 0, s], zdown)
+        send(part.at[p, low], minus.at[p, s], "scatter", rs_r.at[p, 0, s], zdown)
+
+    def scatter_up(p, s):
+        high = (z + 4 - s) % NZ
+        half = block // 2
         if s == 1:
             arrived(plus.at[p, 0, half:], rs_r.at[p, 1, 0], zdown)
             part[p, high, half:] = add(part[p, high, half:], plus[p, 0, half:])
         else:
             arrived(plus.at[p, s - 1], rs_r.at[p, 1, s - 1], zdown)
             part[p, high] = add(part[p, high], plus[p, s - 1])
-        send(part.at[p, high], plus.at[p, s], rs_s.at[p, 1, s], rs_r.at[p, 1, s], zup)
+        send(part.at[p, high], plus.at[p, s], "scatter", rs_r.at[p, 1, s], zup)
 
     def hidden(p):
         arrived(minus.at[p, 3], rs_r.at[p, 0, 3], zup)
@@ -312,8 +324,8 @@
         mine[:, 0:ff] = (back * lift * sigmoid * (1.0 + gate * (1.0 - sigmoid))).astype(BF)
         mine[:, ff : 2 * ff] = (back * active).astype(BF)
         mine[:, 2 * ff :] = value.astype(BF)
-        send(mine, mine, ag_s.at[p, 1, 0], ag_r.at[p, 1, 0], zup)
-        send(mine, mine, ag_s.at[p, 0, 0], ag_r.at[p, 0, 0], zdown)
+        send(mine, mine, "gather", ag_r.at[p, 1, 0], zup)
+        send(mine, mine, "gather", ag_r.at[p, 0, 0], zdown)
         terms = back * value
         high = terms.astype(BF)
         rest = (terms - high.astype(F32)).astype(BF)
@@ -321,32 +333,37 @@
         summed = dot(ones, high, NT) + dot(ones, rest, NT)
         tile_z[p : p + 1, 0:block] = summed[0:1]
 
-    def gather(p, s):
-        low, high = grads.at[p, (z + s) % NZ], grads.at[p, (z - s + NZ) % NZ]
-        half = block // 2
+    def gather_down(p, s):
+        low = grads.at[p, (z + s) % NZ]
         arrived(low, ag_r.at[p, 0, s - 1], zup)
-        if s < 3:
-            send(low, low, ag_s.at[p, 0, s], ag_r.at[p, 0, s], zdown)
-        else:
-            first = grads.at[p, (z + s) % NZ, 0:half]
-            send(first, first, ag_s.at[p, 0, s], ag_r.at[p, 0, s], zdown)
+        if s == 3:
+            low = grads.at[p, (z + s) % NZ, 0 : block // 2]
+        send(low, low, "gather", ag_r.at[p, 0, s], zdown)
+
+    def gather_up(p, s):
+        high = grads.at[p, (z - s + NZ) % NZ]
         arrived(high, ag_r.at[p, 1, s - 1], zdown)
-        if s < 3:
-            send(high, high, ag_s.at[p, 1, s], ag_r.at[p, 1, s], zup)
-        else:
-            last = grads.at[p, (z - s + NZ) % NZ, half:]
-            send(last, last, ag_s.at[p, 1, s], ag_r.at[p, 1, s], zup)
+        if s == 3:
+            high = grads.at[p, (z - s + NZ) % NZ, block // 2 :]
+        send(high, high, "gather", ag_r.at[p, 1, s], zup)
+
+    gathered = set()
+
+    def all_gathered(p):
+        if p not in gathered:
+            gathered.add(p)
+            half = block // 2
+            arrived(grads.at[p, (z + 4) % NZ, 0:half], ag_r.at[p, 0, 3], zup)
+            arrived(grads.at[p, (z + 4) % NZ, half:], ag_r.at[p, 1, 3], zdown)
 
     def tokens(p):
-        half = block // 2
-        arrived(grads.at[p, (z + 4) % NZ, 0:half], ag_r.at[p, 0, 3], zup)
-        arrived(grads.at[p, (z + 4) % NZ, half:], ag_r.at[p, 1, 3], zdown)
+        all_gathered(p)
         for k in (1, 0):
             both = grads[p, k * NY : (k + 1) * NY].reshape(NY * block, 3 * ff)
             value = dot(both[:, :ff], w_gate[...], NT) + dot(both[:, ff : 2 * ff], w_up[...], NT)
             tokens_out[p, k] = value.astype(BF).reshape(NY, block, width)
             if k == 1:
-                send(tokens_out.at[p, 1], sibling_in.at[p], t_s.at[p], t_r.at[p], other)
+                send(tokens_out.at[p, 1], sibling_in.at[p], "terms", t_r.at[p], other)
 
     stores = [
         pltpu.make_async_copy(src, dst, out_s.at[i])
@@ -356,15 +373,16 @@
     ]
 
     def weights(p):
+        all_gathered(p)
         both = grads[p].reshape(count, 3 * ff)
         in_rows = rows[p, 0].reshape(count, width)
         in_grads = rows[p, 1].reshape(count, width)
         gate = dot(in_rows, both[:, :ff], TN)
         lift = dot(in_rows, both[:, ff : 2 * ff], TN)
         drop = dot(both[:, 2 * ff :], in_grads, TN)
-        if p == ORDER[0]:
+        if p == weight_groups[0]:
             acc_gate[...], acc_up[...], acc_down[...] = gate, lift, drop
-        elif p != ORDER[-1]:
+        elif p != weight_groups[-1]:
             acc_gate[...] += gate
             acc_up[...] += lift
             acc_down[...] += drop
@@ -379,37 +397,37 @@
         half = block // 2
         arrived(sibling_in.at[p], t_r.at[p], other)
         tokens_out[p, 0] = add(tokens_out[p, 0], sibling_in[p])
-        send(tokens_out.at[p, 0, 3, 0:half], far_in.at[p, 0], yr_s.at[p, 0], yr_r.at[p, 0], up)
-        send(tokens_out.at[p, 0, 3, half:], far_in.at[p, 1], yr_s.at[p, 1], yr_r.at[p, 1], down)
-
-    def relay(p):
+        send(tokens_out.at[p, 0, 3, 0:half], far_in.at[p, 0], "sums", yr_r.at[p, 0], up)
+        send(tokens_out.at[p, 0, 3, half:], far_in.at[p, 1], "sums", yr_r.at[p, 1], down)
+
+    def relay_up(p):
         half = block // 2
         arrived(far_in.at[p, 0], yr_r.at[p, 0], down)
         tokens_out[p, 0, 1, 0:half] = add(tokens_out[p, 0, 1, 0:half], far_in[p, 0])
-        send(tokens_out.at[p, 0, 1], near_in.at[p, 0], yr_s.at[p, 2], yr_r.at[p, 2], up)
+        send(tokens_out.at[p, 0, 1], near_in.at[p, 0], "sums", yr_r.at[p, 2], up)
+
+    def relay_down(p):
+        half = block // 2
         arrived(far_in.at[p, 1], yr_r.at[p, 1], up)
         tokens_out[p, 0, 2, half:] = add(tokens_out[p, 0, 2, half:], far_in[p, 1])
-        send(tokens_out.at[p, 0, 2], near_in.at[p, 1], yr_s.at[p, 3], yr_r.at[p, 3], down)
+        send(tokens_out.at[p, 0, 2], near_in.at[p, 1], "sums", yr_r.at[p, 3], down)
 
     def finish(p):
         arrived(near_in.at[p, 0], yr_r.at[p, 2], down)
         arrived(near_in.at[p, 1], yr_r.at[p, 3], up)
         value = tokens_out[p, 0, 0].astype(F32) + near_in[p, 0].astype(F32) + near_in[p, 1].astype(F32)
-        final[p] = value.reshape(NZ, CAP, width).astype(BF)
+        final[p * NZ : (p + 1) * NZ] = value.reshape(NZ, CAP, width).astype(BF)
         for dz in steps_z:
             if (dz, p) != (0, 0):
-                send(
-                    final.at[p, (z + dz) % NZ], table.at[z, x],
-                    back_s.at[p, dz], back_r.at[(-p) % NX, (-dz) % NZ], at(dz, p),
-                )
+                send(final.at[p * NZ + (z + dz) % NZ], table.at[z, x], "back", back_r, at(dz, p))
             else:
-                table[z, x] = final[p, z]
+                table[z, x] = final[z]
 
     others_z = range(1, NZ)
 
     def router_start():
         for dz in others_z:
-            send(tile_z, tile_zin.at[z], r0_s.at[dz], r0_r.at[(-dz) % NZ], at(dz))
+            send(tile_z, tile_zin.at[z], "rz", router_r.at[0], at(dz))
         tile_zin[z] = tile_z[...]
 
     def three_parts(value):
@@ -428,8 +446,7 @@
     in_slot = jnp.bitwise_and(row, CAP - 1)
 
     def router_local():
-        for dz in others_z:
-            arrived(tile_zin.at[(z + dz) % NZ], r0_r.at[dz], at(dz))
+        arrived(tile_zin.at[1:NZ], router_r.at[0], zup)
         total = jnp.zeros((8, 128), F32)
         inside = lax.broadcasted_iota(jnp.int32, (8, 128), 1) < block
         for p in range(NX):
@@ -439,54 +456,63 @@
         tile[...] = total
         for k, g in around:
             i = NY * k + g
-            send(tile, tile_in.at[i], r1_s.at[i], r1_r.at[i], at(dy=GROUP_Y[g], dc=k))
+            send(tile, tile_in.at[i], "ry", router_r.at[1], at(dy=GROUP_Y[g], dc=k))
 
     def router_x():
         summed = tile[0:1, :]
+        arrived(tile_in.at[1 : NY * NC], router_r.at[1], other)
         for k, g in around:
             i = NY * k + g
-            arrived(tile_in.at[i], r1_r.at[i], other)
             summed = summed + tile_in[i, i : i + 1, :]
         wide = jnp.broadcast_to(summed, (8, 128))
         for dx in range(NX):
             tile_x[dx] = moved(wide, jnp.right_shift(row, 3) == dx, column == x * CAP + in_slot)
         router[x] = tile_x[0]
         for dx in range(1, NX):
-            send(tile_x.at[dx], router.at[x], r2_s.at[dx], r2_r.at[(-dx) % NX], at(dx=dx))
+            send(tile_x.at[dx], router.at[x], "rx", router_r.at[2], at(dx=dx))
 
     todo = {
-        "take": take, "pass_on": pass_on, "near": near, "far": far, "products": products,
-        "hidden": hidden, "tokens": tokens, "weights": weights, "join": join, "relay": relay,
-        "finish": finish,
+        "take": take, "products": products, "hidden": hidden, "tokens": tokens, "weights": weights,
+        "pass_tokens": pass_tokens, "pass_grads": pass_grads,
+        "near_grads": functools.partial(keep, g=1, h=1),
+        "near_tokens": functools.partial(keep, g=2, h=0),
+        "far_tokens": functools.partial(keep, g=3, h=0),
+        "far_grads": functools.partial(keep, g=3, h=1),
+        "join": join, "relay_up": relay_up, "relay_down": relay_down, "finish": finish,
     }
     for s in (1, 2, 3):
-        todo[f"scatter_{s}"] = functools.partial(scatter, s=s)
-        todo[f"gather_{s}"] = functools.partial(gather, s=s)
-    plan = [
-        (start + place * GAP, place, stage, p)
-        for place, p in enumerate(ORDER)
-        for stage, start in STAGES
-    ]
-    last = {stage: start + (NX - 1) * GAP for stage, start in STAGES}
-    plan.append((last["hidden"] + 0.1, NX, router_start, None))
-    plan.append((last["gather_2"] + 0.1, NX, router_local, None))
-    plan.append((last["tokens"] + 0.1, NX, router_x, None))
-    for _, _, stage, p in sorted(plan, key=lambda item: item[:2]):
-        if p is None:
-            stage()
-        else:
-            todo[stage](p)
-
-    for dx in range(1, NX):
-        arrived(router.at[(x + dx) % NX], r2_r.at[dx], at(dx=dx))
-    for p in ORDER:
-        for dz in range(NZ):
-            if (dz, p) != (0, 0):
-                arrived(table.at[(z + dz) % NZ, (x + p) % NX], back_r.at[p, dz], at(dz, p))
+        todo[f"scatter_down_{s}"] = functools.partial(scatter_down, s=s)
+        todo[f"scatter_up_{s}"] = functools.partial(scatter_up, s=s)
+        todo[f"gather_down_{s}"] = functools.partial(gather_down, s=s)
+        todo[f"gather_up_{s}"] = functools.partial(gather_up, s=s)
+    plan = sorted(
+        (place, stage, p) for stage, *places in STAGES for place, p in zip(places, ORDER)
+    )
+    weight_groups = [p for _, stage, p in plan if stage == "weights"]
+    last = {stage: max(places) for stage, *places in STAGES}
+    after = {
+        last["hidden"]: router_start, last["gather_down_2"]: router_local, last["tokens"]: router_x
+    }
+    for place, stage, p in plan:
+        todo[stage](p)
+        if place in after:
+            after[place]()
+
+    arrived(tile_x.at[1:NX], router_r.at[2], at(dx=1))
+    arrived(final.at[1:], back_r, zup)
     for copy in stores:
         copy.wait()
-    for copy in sends:
-        copy.wait_send()
+    all_sent("a2a", packed.at[1:])
+    all_sent("y", rows.at[:, :, 0, 1:])
+    all_sent("sibling", rows.at[:, :, 1])
+    all_sent("scatter", part.at[:, 1:])
+    all_sent("gather", grads.at[:, 1:])
+    all_sent("terms", sibling_in)
+    all_sent("sums", tokens_out.at[:, 0, 1:])
+    all_sent("back", final.at[1:])
+    all_sent("rz", tile_zin.at[1:])
+    all_sent("ry", tile_in.at[1:])
+    all_sent("rx", tile_x.at[1:])
 
 
 def experts(routes, probs, tokens, cotangent, w_gate, w_up, w_down):
@@ -510,15 +536,14 @@
         in_specs=[vmem] * 2 + [free] * 5,
         out_specs=(vmem,) * 3 + (free,) * 3,
         scratch_shapes=[
-            pltpu.VMEM((NZ, count, width), BF),
-            pltpu.VMEM((NZ, count, width), BF),
+            pltpu.VMEM((NZ, 2, count, width), BF),
             pltpu.VMEM((width, ff), BF),
             pltpu.VMEM((width, ff), BF),
             pltpu.VMEM((ff, width), BF),
             pltpu.VMEM((width, ff), BF),
             pltpu.VMEM((width, ff), BF),
             pltpu.VMEM((ff, width), BF),
-            pltpu.VMEM((NZ, NX, 2 * CAP, width), BF),
+            pltpu.VMEM((NZ * NX, 2 * CAP, width), BF),
             pltpu.VMEM((NX, NZ, 2 * CAP, width), BF),
             pltpu.VMEM((NX, 2, NC, NY, block, width), BF),
             pltpu.VMEM((NX, NZ, block, 3 * ff), BF),
@@ -529,7 +554,7 @@
             pltpu.VMEM((NX, NY, block, width), BF),
             pltpu.VMEM((NX, 2, block, width), BF),
             pltpu.VMEM((NX, 2, block // 2, width), BF),
-            pltpu.VMEM((NX, NZ, CAP, width), BF),
+            pltpu.VMEM((NX * NZ, CAP, width), BF),
             pltpu.VMEM((width, ff), F32),
             pltpu.VMEM((width, ff), F32),
             pltpu.VMEM((ff, width), F32),
@@ -538,10 +563,8 @@
             pltpu.VMEM((8, 128), F32),
             pltpu.VMEM((8, 8, 128), F32),
             pltpu.VMEM((NX, 8, 128), F32),
-            dma(NX, NZ), dma(NX, NZ), dma(NX, NY, 2), dma(NX, NY, 2), dma(NX, NY, 2), dma(NX, NY, 2),
-            dma(NX, 2, 4), dma(NX, 2, 4), dma(NX, 2, 4), dma(NX, 2, 4),
-            dma(NX), dma(NX), dma(NX, 4), dma(NX, 4),
-            dma(NX, NZ), dma(NX, NZ), dma(2, NZ), dma(3), dma(3), dma(NZ), dma(NZ), dma(8), dma(8), dma(NX), dma(NX),
+            dma(11), dma(NX), dma(NX, 3, 2), dma(NX), dma(NX, 2, 4), dma(NX, 2, 4), dma(NX), dma(NX, 4),
+            pltpu.SemaphoreType.DMA, dma(NZ), dma(3), dma(3), dma(3),
         ],
         compiler_params=pltpu.CompilerParams(
             collective_id=0, has_side_effects=True, vmem_limit_bytes=56 * MIB

time: 138 us -> 128 us (0.928); the launches traced: 135 us -> 127 us
  Pallas kernels: 134 us -> 127 us
    pallas_call x1, Pallas kernels: 129 us -> 121 us  [experts(): pl.pallas_call(expert_kernel, out_shape=(jax.ShapeDtypeStruct((NX * CAP,...]
where the time goes in v2:
time: 128 us; the launch traced here: 127 us
  Pallas kernels  127 us (99%)
    pallas_call x1, Pallas kernels, experts(): pl.pallas_call(expert_kernel, out_shape=(jax.ShapeDtypeStruct((NX * CAP,...  121 us
    pallas_call x1, Pallas kernels, unpack(): pl.pallas_call(unpack_kernel, out_shape=(jax.ShapeDtypeStruct((rows, NZ *...  5.5 us

profile of v2, /device:TPU:1, one launch (start us, length us, event | category | flops | bytes accessed | tf_op | source)
XLA Modules:
  0.0 127.2 jit_solution(12380412231201369779)
XLA Ops:
  0.6 121.0 %shard_map.110 = (bf16[32,256]{1,0:T(8,128)(2,1)}, bf16[8,4,8,896]{3,2,1,0:T(8,128)(2,1)}, f32[4,8,128]{2,1,0:T(8,128)}, bf16[896,256]{1,0:T(8,128)(2,1)}, bf16[...) custom-call(s32[8,256]{1,0:T(8,128)} %bitcast.6, bf16[8,256]{1,0:T(8,128)(2,1)} %bitcast.8, bf16[256,7168]{1,0:T(8,128)(2,1)} %tokens_in.1, ...), custom_call_target="tpu_custom_call" | custom-call | flops 7516192768 | bytes 16777216 | tf_op jit(solution)/shard_map/pallas_call | solution.py:526
  121.7 5.5 %shard_map.111 = (bf16[256,7168]{1,0:T(8,128)(2,1)}, f32[8,256]{1,0:T(8,128)}, bf16[1,896,256]{2,1,0:T(8,128)(2,1)}, bf16[1,896,256]{2,1,0:T(8,128)(2,1)}, bf16[1,256,896]{2,1,0:T(8,128)(2,1)}) custom-call(s32[8,256]{1,0:T(8,128)} %bitcast.7, bf16[8,256]{1,0:T(8,128)(2,1)} %bitcast.9, bf16[32,256]{1,0:T(8,128)(2,1)} %get-tuple-element.16.choice, ...), custom_call_target="tpu_custom_call" | custom-call | tf_op jit(solution)/shard_map/pallas_call | solution.py:96

commit v3 on v2

--- a/solution.py
+++ b/solution.py
@@ -45,7 +45,7 @@
 def unpack_kernel(
     routes, probs, choice, table, router, gate_in, up_in, down_in,
     token_grad, router_grad, gate_out, up_out, down_out,
-    result, gate_v, up_v, down_v, result_s, load_s, grad_s,
+    slots_v, result, gate_v, up_v, down_v, result_s, load_s, grad_s,
 ):
     top, rows = routes.shape
     slots = NX * CAP
@@ -64,8 +64,11 @@
     chosen = choice[...]
     for d in range(NZ):
         rows_in = table[d].astype(F32).reshape(slots, width).astype(BF)
-        result[d] = dot(chosen, rows_in, TN).astype(BF)
-        copy(result.at[d], token_grad.at[:, d * width : (d + 1) * width], result_s.at[d])
+        slots_v[:, d * width : (d + 1) * width] = rows_in
+    some = result.shape[1]
+    for r in range(result.shape[0]):
+        result[r] = dot(chosen[:, r * some : (r + 1) * some], slots_v[...], TN).astype(BF)
+        copy(result.at[r], token_grad.at[r * some : (r + 1) * some], result_s.at[r])
 
     for i, (_, v, dst) in enumerate(through):
         loads[i].wait()
@@ -105,7 +108,8 @@
         in_specs=[vmem] * 5 + [free] * 3,
         out_specs=(free, vmem, free, free, free),
         scratch_shapes=[
-            pltpu.VMEM((NZ, rows, part), BF),
+            pltpu.VMEM((NX * CAP, NZ * part), BF),
+            pltpu.VMEM((4, rows // 4, NZ * part), BF),
             pltpu.VMEM((width, ff), BF),
             pltpu.VMEM((width, ff), BF),
             pltpu.VMEM((ff, width), BF),
@@ -252,28 +256,29 @@
         for h in range(2):
             send(rows.at[p, h, 0, 0], rows.at[p, h, 0, 1], "y", y_r.at[p, 0, h], down)
             send(rows.at[p, 1 - h, 0, 0], rows.at[p, 1 - h, 0, 2], "y", y_r.at[p, 1, 1 - h], up)
-        for h in range(2):
-            to_sibling(p, 0, h)
-
-    def to_sibling(p, g, h):
-        send(rows.at[p, h, 0, g], rows.at[p, h, 1, g], "sibling", sib_r.at[p], other)
+        to_sibling(p, 0, 1)
+
+    def to_sibling(p, first, last):
+        send(
+            rows.at[p, :, 0, first:last], rows.at[p, :, 1, first:last], "sibling", sib_r.at[p], other
+        )
+
+    left = {p: {1: 4, 3: 2} for p in ORDER}
 
     def from_y(p, g, h):
         arrived(rows.at[p, h, 0, g], y_r.at[p, g - 1, h], up)
+        first, last = (3, 4) if g == 3 else (1, 3)
+        left[p][first] -= 1
+        if left[p][first] == 0:
+            to_sibling(p, first, last)
 
     def pass_tokens(p):
         from_y(p, 1, 0)
         send(rows.at[p, 0, 0, 1], rows.at[p, 0, 0, 3], "y", y_r.at[p, 2, 0], down)
-        to_sibling(p, 1, 0)
 
     def pass_grads(p):
         from_y(p, 2, 1)
         send(rows.at[p, 1, 0, 2], rows.at[p, 1, 0, 3], "y", y_r.at[p, 2, 1], up)
-        to_sibling(p, 2, 1)
-
-    def keep(p, g, h):
-        from_y(p, g, h)
-        to_sibling(p, g, h)
 
     def products(p):
         arrived(rows.at[p, :, 1], sib_r.at[p], other)
@@ -474,10 +479,10 @@
     todo = {
         "take": take, "products": products, "hidden": hidden, "tokens": tokens, "weights": weights,
         "pass_tokens": pass_tokens, "pass_grads": pass_grads,
-        "near_grads": functools.partial(keep, g=1, h=1),
-        "near_tokens": functools.partial(keep, g=2, h=0),
-        "far_tokens": functools.partial(keep, g=3, h=0),
-        "far_grads": functools.partial(keep, g=3, h=1),
+        "near_grads": functools.partial(from_y, g=1, h=1),
+        "near_tokens": functools.partial(from_y, g=2, h=0),
+        "far_tokens": functools.partial(from_y, g=3, h=0),
+        "far_grads": functools.partial(from_y, g=3, h=1),
         "join": join, "relay_up": relay_up, "relay_down": relay_down, "finish": finish,
     }
     for s in (1, 2, 3):

time: 128 us -> 127 us (level)
  no operation moved by 1% of the time
where the time goes in v3:
time: 127 us; the launch traced here: 126 us
  Pallas kernels  126 us (99%)
    pallas_call x1, Pallas kernels, experts(): pl.pallas_call(expert_kernel, out_shape=(jax.ShapeDtypeStruct((NX * CAP,...  121 us
    pallas_call x1, Pallas kernels, unpack(): pl.pallas_call(unpack_kernel, out_shape=(jax.ShapeDtypeStruct((rows, NZ *...  4.46 us

profile of v3, /device:TPU:1, one launch (start us, length us, event | category | flops | bytes accessed | tf_op | source)
XLA Modules:
  0.0 126.4 jit_solution(10935163331850571268)
XLA Ops:
  0.6 121.3 %shard_map.110 = (bf16[32,256]{1,0:T(8,128)(2,1)}, bf16[8,4,8,896]{3,2,1,0:T(8,128)(2,1)}, f32[4,8,128]{2,1,0:T(8,128)}, bf16[896,256]{1,0:T(8,128)(2,1)}, bf16[...) custom-call(s32[8,256]{1,0:T(8,128)} %bitcast.6, bf16[8,256]{1,0:T(8,128)(2,1)} %bitcast.8, bf16[256,7168]{1,0:T(8,128)(2,1)} %tokens_in.1, ...), custom_call_target="tpu_custom_call" | custom-call | flops 7516192768 | bytes 16777216 | tf_op jit(solution)/shard_map/pallas_call | solution.py:531
  122.0 4.5 %shard_map.111 = (bf16[256,7168]{1,0:T(8,128)(2,1)}, f32[8,256]{1,0:T(8,128)}, bf16[1,896,256]{2,1,0:T(8,128)(2,1)}, bf16[1,896,256]{2,1,0:T(8,128)(2,1)}, bf16[1,256,896]{2,1,0:T(8,128)(2,1)}) custom-call(s32[8,256]{1,0:T(8,128)} %bitcast.7, bf16[8,256]{1,0:T(8,128)(2,1)} %bitcast.9, bf16[32,256]{1,0:T(8,128)(2,1)} %get-tuple-element.16.choice, ...), custom_call_target="tpu_custom_call" | custom-call | tf_op jit(solution)/shard_map/pallas_call | solution.py:99
